TPU v7x, 512 devices: a whole 4x8x8 slice. The times are simulated.
512 devices in a mesh: seq: 64 (over x, y, core), head: 8 (over z).
Axes of the slice: x: 4, y: 8, z: 8, core: 2. Of those that a mesh axis runs over, the one named last changes fastest.
Arguments:
- queries: bfloat16 [65536, 4096], P(('seq', 'head')), may hold values from -80 to 80
- keys: bfloat16 [65536, 512], P(('seq', 'head')), may hold values from -4 to 4
- values: bfloat16 [65536, 512], P(('seq', 'head')), may hold values from -6 to 6
- output_gradient: bfloat16 [65536, 4096], P(('seq', 'head')), may hold values from -0.59765625 to 0.59765625
- inputs: bfloat16 [65536, 8192], P(('seq', 'head')), may hold values from -6 to 6
- adapter_activation: bfloat16 [65536, 16], P(('seq', 'head')), may hold values from -6 to 6
- adapter_up_weight: bfloat16 [64, 16, 4096], P('seq', None, 'head'), may hold values from -0.09375 to 0.09375
- segment_length: int32 [64, 8], P('seq'), may hold values from 1 to 384, 1024 in all within a row
- segment_adapter: int32 [64, 8], P('seq'), may hold values from 0 to 63
- owner: int32 [64], replicated, may hold values from 0 to 63, each once
Outputs:
- down_gradient: float32 [64, 8192, 16], P('seq', 'head')
- up_gradient: float32 [64, 16, 4096], P('seq', None, 'head')
Inputs may be any that keep to these rules, and one draw needn't show every extreme that they name: `segment_length`: each pack's 8 lengths sum to 1024, and its longest segment has exactly 384 tokens. `owner`: each seq index owns exactly one adapter.
All inputs are finite; a program needn't handle non-finite values.
Results may differ from a plain program's by a relative error of at most 0.014.
Values may be sent and summed in bfloat16 or wider, within the bound.
A program may use at most 64 MiB of HBM per device.

v0:
```python
import jax
import jax.numpy as jnp
from jax import lax
from jax.sharding import PartitionSpec as P

QUERY_HEADS = 32
KEY_VALUE_HEADS = 4
HEAD_SIZE = 128


ADAPTER_SCALE = 2.0
HIGHEST = lax.Precision.HIGHEST


def segment_of(seg_lens, pack_len):
    seg_ends = jnp.cumsum(seg_lens)
    positions = jnp.arange(pack_len, dtype=jnp.int32)
    return jnp.sum((positions[:, None] >= seg_ends[None, :]).astype(jnp.int32), axis=1)


def head_backward(q_head, g_head, k_head, v_head, segment, block_rows):
    pack_len, head_width = q_head.shape
    score_scale = 1.0 / head_width**0.5
    positions = jnp.arange(pack_len, dtype=jnp.int32)

    def one_block(starting_row):
        q_rows = lax.dynamic_slice_in_dim(q_head, starting_row, block_rows, 0)
        g_rows = lax.dynamic_slice_in_dim(g_head, starting_row, block_rows, 0)
        row_seg = lax.dynamic_slice_in_dim(segment, starting_row, block_rows, 0)
        row_pos = starting_row + jnp.arange(block_rows, dtype=jnp.int32)
        scores = (
            jnp.einsum("qd,kd->qk", q_rows, k_head, preferred_element_type=jnp.float32)
            * score_scale
        )
        allowed = (row_seg[:, None] == segment[None, :]) & (positions[None, :] <= row_pos[:, None])
        scores = jnp.where(allowed, scores, -jnp.inf)
        row_max = jnp.max(scores, axis=1, keepdims=True)
        weights = jnp.exp(scores - row_max)
        attn_prob = weights / jnp.sum(weights, axis=1, keepdims=True)
        d_prob = jnp.einsum("qd,kd->qk", g_rows, v_head, preferred_element_type=jnp.float32)
        row_delta = jnp.sum(attn_prob * d_prob, axis=1, keepdims=True)
        dscore = (attn_prob * (d_prob - row_delta) * score_scale).astype(jnp.bfloat16)
        return jnp.dot(dscore, k_head, preferred_element_type=jnp.float32).astype(jnp.bfloat16)

    starts = jnp.arange(pack_len // block_rows, dtype=jnp.int32) * block_rows
    return lax.map(one_block, starts).reshape(pack_len, head_width)


def on_device(
    queries,
    keys,
    values,
    output_gradient,
    inputs,
    adapter_activation,
    adapter_up_weight,
    segment_length,
    segment_adapter,
    owner,
):
    local_head_count = lax.axis_size("head")
    tok_rows = queries.shape[0]
    pack_len = tok_rows * local_head_count
    block_rows = min(512, pack_len)
    resident_heads = QUERY_HEADS // local_head_count
    resident_key_value_heads = max(KEY_VALUE_HEADS // local_head_count, 1)
    q_heads, g_heads = (
        lax.all_to_all(queries, "head", split_axis=1, concat_axis=0, tiled=True),
        lax.all_to_all(output_gradient, "head", split_axis=1, concat_axis=0, tiled=True),
    )
    k_all, v_all = (
        lax.all_gather(keys, "head", axis=0, tiled=True),
        lax.all_gather(values, "head", axis=0, tiled=True),
    )
    first_key_value_head = (
        lax.axis_index("head") * resident_heads // (QUERY_HEADS // KEY_VALUE_HEADS)
    )
    k_local = lax.dynamic_slice_in_dim(
        k_all, first_key_value_head * HEAD_SIZE, resident_key_value_heads * HEAD_SIZE, 1
    )
    v_local = lax.dynamic_slice_in_dim(
        v_all, first_key_value_head * HEAD_SIZE, resident_key_value_heads * HEAD_SIZE, 1
    )
    feat_rows, activation_rows = (
        lax.all_to_all(inputs, "head", split_axis=1, concat_axis=0, tiled=True),
        lax.all_to_all(
            jnp.tile(adapter_activation, (1, local_head_count)),
            "head",
            split_axis=1,
            concat_axis=0,
            tiled=True,
        ),
    )
    segment = segment_of(segment_length[0], pack_len)
    q_stack = q_heads.reshape(pack_len, resident_heads, HEAD_SIZE).transpose(1, 0, 2)
    g_stack = g_heads.reshape(pack_len, resident_heads, HEAD_SIZE).transpose(1, 0, 2)
    k_stack = jnp.repeat(
        k_local.reshape(pack_len, resident_key_value_heads, HEAD_SIZE).transpose(1, 0, 2),
        resident_heads // resident_key_value_heads,
        axis=0,
    )
    v_stack = jnp.repeat(
        v_local.reshape(pack_len, resident_key_value_heads, HEAD_SIZE).transpose(1, 0, 2),
        resident_heads // resident_key_value_heads,
        axis=0,
    )
    dq_stack = lax.map(
        lambda stacked: head_backward(
            stacked[0], stacked[1], stacked[2], stacked[3], segment, block_rows
        ),
        (q_stack, g_stack, k_stack, v_stack),
    )
    dquery = dq_stack.transpose(1, 0, 2).reshape(pack_len, resident_heads * HEAD_SIZE)
    segment_index = segment_adapter[0]
    seg_total = segment_index.shape[0]
    adapter_total = owner.shape[0]
    adapter_rank_width = adapter_up_weight.shape[1]
    query_width = dquery.shape[1]
    d_width = feat_rows.shape[1]
    adapter_cols = jnp.arange(adapter_total, dtype=jnp.int32)
    seg_mask = segment[:, None] == jnp.arange(seg_total, dtype=jnp.int32)[None, :]
    seg_hits = segment_index[:, None] == adapter_cols[None, :]
    up_weight_every_token = lax.all_gather(adapter_up_weight, "seq", axis=0, tiled=True).reshape(
        adapter_total, adapter_rank_width * query_width
    )
    up_weight_segment = jnp.dot(
        seg_hits.astype(jnp.bfloat16), up_weight_every_token, preferred_element_type=jnp.float32
    ).astype(jnp.bfloat16)
    rank_seg = jnp.einsum(
        "tf,cf->tc",
        dquery,
        up_weight_segment.reshape(seg_total * adapter_rank_width, query_width),
        preferred_element_type=jnp.float32,
    )
    rank_part = jnp.sum(
        rank_seg.reshape(pack_len, seg_total, adapter_rank_width) * seg_mask[:, :, None], axis=1
    )
    rank_low = lax.psum(rank_part, "head").astype(jnp.bfloat16)
    mask_low = seg_mask.astype(jnp.bfloat16)
    seg_owner = jnp.sum(jnp.where(seg_hits, owner[None, :], 0), axis=1)
    slot_map = (seg_owner[:, None] == adapter_cols[None, :]).astype(jnp.float32)
    rank_cols = (mask_low[:, :, None] * rank_low[:, None, :]).reshape(
        pack_len, seg_total * adapter_rank_width
    )
    act_cols = (mask_low[:, :, None] * activation_rows[:, None, :]).reshape(
        pack_len, seg_total * adapter_rank_width
    )
    part_a = jnp.einsum(
        "td,tc->dc", feat_rows, rank_cols, preferred_element_type=jnp.float32
    ).reshape(d_width, seg_total, adapter_rank_width)
    part_b = jnp.einsum("tc,tf->cf", act_cols, dquery, preferred_element_type=jnp.float32).reshape(
        seg_total, adapter_rank_width, query_width
    )
    slot_cols = slot_map
    parts_a = lax.all_to_all(
        jnp.einsum("dsr,so->odr", part_a, slot_cols, precision=HIGHEST),
        "seq",
        split_axis=0,
        concat_axis=0,
        tiled=True,
    )
    slot_cols = slot_map
    parts_b = lax.all_to_all(
        jnp.einsum("srf,so->orf", part_b, slot_cols, precision=HIGHEST),
        "seq",
        split_axis=0,
        concat_axis=0,
        tiled=True,
    )
    down_gradient = jnp.sum(parts_a, axis=0, keepdims=True)
    up_gradient = jnp.sum(parts_b, axis=0, keepdims=True)
    return (down_gradient * ADAPTER_SCALE, up_gradient * ADAPTER_SCALE)


def solution(mesh):
    return jax.shard_map(
        on_device,
        mesh=mesh,
        in_specs=(
            P(("seq", "head"), None),
            P(("seq", "head"), None),
            P(("seq", "head"), None),
            P(("seq", "head"), None),
            P(("seq", "head"), None),
            P(("seq", "head"), None),
            P("seq", None, "head"),
            P("seq", None),
            P("seq", None),
            P(),
        ),
        out_specs=(P("seq", "head", None), P("seq", None, "head")),
        check_vma=False,
    )
```

profile of v0, /device:TPU:1, one launch (start us, length us, event | category | flops | bytes accessed | tf_op | source)
XLA Modules:
  0.0 406.9 jit_solution(16149362904592485424)
XLA Ops:
  7.9 1.3 tile.2
  9.2 10.9 %all-to-all-start.4 = ((bf16[128,8,16]{0,2,1:T(8,128)(2,1)}), bf16[128,8,16]{0,2,1:T(8,128)(2,1)S(1)}, u32[]{:S(2)}, u32[]{:S(2)}) async-start(bf16[128,8,16]{0,2,1:T(8,128)(2,1)} %tile.2), calls=%async_computation.4 | async-start | bytes 65536 | tf_op jit(solution)/shard_map/all_to_all | solution.py:86
  20.1 2.3 copy.69
  22.4 4.5 %all-to-all-done.4 = bf16[128,8,16]{0,2,1:T(8,128)(2,1)S(1)} async-done(((bf16[128,8,16]{0,2,1:T(8,128)(2,1)}), bf16[128,8,16]{0,2,1:T(8,128)(2,1)S(1)}, u32[]{:S(2)}, u32[]{:S(2)}) %all-to-all-start.4) | async-done | bytes 32800 | tf_op jit(solution)/shard_map/all_to_all | solution.py:86
  26.9 3.6 all-to-all-start
  31.3 1.3 copy.71
  32.6 33.6 %all-to-all-done = bf16[128,8,512]{0,2,1:T(8,128)(2,1)S(1)} async-done(((bf16[128,8,512]{0,2,1:T(8,128)(2,1)}), bf16[128,8,512]{0,2,1:T(8,128)(2,1)S(1)}, u32[]{:S(2)}, u32[]{:S(2)}) %all-to-all-start) | async-done | bytes 1048608 | tf_op jit(solution)/shard_map/all_to_all | solution.py:68
  66.2 3.6 all-to-all-start.1
  70.8 4.1 %copy.78 = bf16[128,8192]{0,1:T(8,128)(2,1)} copy(bf16[128,8192]{1,0:T(8,128)(2,1)} %param.18) | data formatting | bytes 4194304 | tf_op args[4]
  77.6 1.3 reshape.172
  78.9 22.7 %all-to-all-done.1 = bf16[128,8,512]{0,2,1:T(8,128)(2,1)S(1)} async-done(((bf16[128,8,512]{0,2,1:T(8,128)(2,1)}), bf16[128,8,512]{0,2,1:T(8,128)(2,1)S(1)}, u32[]{:S(2)}, u32[]{:S(2)}) %all-to-all-start.1) | async-done | bytes 1048608 | tf_op jit(solution)/shard_map/all_to_all | solution.py:69
  101.5 4.3 %all-to-all-start.2 = ((bf16[128,8,1024]{0,2,1:T(8,128)(2,1)}), bf16[128,8,1024]{0,2,1:T(8,128)(2,1)}, u32[]{:S(2)}, u32[]{:S(2)}) async-start(bf16[128,8,1024]{0,2,1:T(8,128)(2,1)} %bitcast.20), calls=%async_computation.2 | async-start | bytes 4194304 | tf_op jit(solution)/shard_map/all_to_all | solution.py:85
  106.6 1.3 reshape.173
  107.8 1.0 constant_dynamic-slice_fusion.3
  108.8 2.8 all-gather.6.cloned.1.call-done
  111.6 1.0 constant_dynamic-slice_fusion.2
  112.8 59.6 %while.22 = (s32[]{:T(128)}, bf16[4,1024,128]{1,2,0:T(8,128)(2,1)}, bf16[4,1024,128]{1,2,0:T(8,128)(2,1)}, bf16[4,1024,128]{1,2,0:T(8,128)(2,1)}, bf16[4,1024,12...) while((s32[]{:T(128)}, bf16[4,1024,128]{1,2,0:T(8,128)(2,1)}, ...), condition=%wide.region_9.10_spmd, body=%wide.region_3.9_spmd.sunk | while | flops 412154880 | bytes 17990548 | solution.py:107
  112.8 1.1 constant_dynamic-slice_fusion.5
  114.3 12.5 %while.23 = (s32[]{:T(128)}, bf16[2,512,128]{2,1,0:T(8,128)(2,1)S(1)}, s32[2]{0:T(128)S(1)}, s32[1024]{0:T(1024)S(1)}, bf16[1024,128]{1,0:T(8,128)(2,1)S(1)}, /*...) while((s32[]{:T(128)}, ...), condition=%wide.region_8.8_spmd.clone, body=%wide.region_4.7_spmd.clone.sunk | while | flops 412154880 | bytes 13795503 | solution.py:46
  119.7 0.9 fusion.54
  126.0 0.9 fusion.54
  127.7 1.1 constant_dynamic-slice_fusion.5
  129.2 12.5 %while.23 = (s32[]{:T(128)}, bf16[2,512,128]{2,1,0:T(8,128)(2,1)S(1)}, s32[2]{0:T(128)S(1)}, s32[1024]{0:T(1024)S(1)}, bf16[1024,128]{1,0:T(8,128)(2,1)S(1)}, /*...) while((s32[]{:T(128)}, ...), condition=%wide.region_8.8_spmd.clone, body=%wide.region_4.7_spmd.clone.sunk | while | flops 412154880 | bytes 13795503 | solution.py:46
  134.6 0.9 fusion.54
  139.0 0.7 fusion.52
  140.9 0.8 fusion.54
  142.6 1.1 constant_dynamic-slice_fusion.5
  144.1 12.5 %while.23 = (s32[]{:T(128)}, bf16[2,512,128]{2,1,0:T(8,128)(2,1)S(1)}, s32[2]{0:T(128)S(1)}, s32[1024]{0:T(1024)S(1)}, bf16[1024,128]{1,0:T(8,128)(2,1)S(1)}, /*...) while((s32[]{:T(128)}, ...), condition=%wide.region_8.8_spmd.clone, body=%wide.region_4.7_spmd.clone.sunk | while | flops 412154880 | bytes 13795503 | solution.py:46
  149.5 0.9 fusion.54
  155.8 0.9 fusion.54
  157.5 1.1 constant_dynamic-slice_fusion.5
  159.0 12.5 %while.23 = (s32[]{:T(128)}, bf16[2,512,128]{2,1,0:T(8,128)(2,1)S(1)}, s32[2]{0:T(128)S(1)}, s32[1024]{0:T(1024)S(1)}, bf16[1024,128]{1,0:T(8,128)(2,1)S(1)}, /*...) while((s32[]{:T(128)}, ...), condition=%wide.region_8.8_spmd.clone, body=%wide.region_4.7_spmd.clone.sunk | while | flops 412154880 | bytes 13795503 | solution.py:46
  164.4 0.9 fusion.54
  170.7 0.8 fusion.54
  172.4 27.0 %all-gather.8.cloned.1.call-done = bf16[64,16,512]{2,1,0:T(8,128)(2,1)} async-done(((bf16[1,16,512]{2,1,0:T(8,128)(2,1)}), bf16[64,16,512]{2,1,0:T(8,128)(2,1)}) %all-gather.8.cloned.1.call-update) | async-done | bytes 1048592 | tf_op jit(solution)/shard_map/all_gather | solution.py:123
  199.4 1.8 copy.95
  201.9 24.1 %psum.7 = bf16[1024,16]{0,1:T(8,128)(2,1)S(1)} all-reduce(f32[1024,16]{0,1:T(8,128)S(1)} %fusion.16), channel_id=1, replica_groups=mesh['seq'=64,'head'=8] {'head'}, use_global_device_ids=true, to_apply=%region_11.12 | all-reduce | flops 16384 | bytes 98304 | tf_op jit(solution)/shard_map/psum | solution.py:138
  226.6 1.1 fusion.25
  227.7 2.5 copy.85
  230.2 14.0 %all-to-all-start.5 = ((f32[64,16,512]{2,1,0:T(8,128)}), f32[64,16,512]{2,1,0:T(8,128)S(1)}, u32[]{:S(2)}, u32[]{:S(2)}) async-start(f32[64,16,512]{2,1,0:T(8,128)} %copy.85), calls=%async_computation.5 | async-start | bytes 4194304 | tf_op jit(solution)/shard_map/all_to_all | solution.py:163
  244.2 3.9 copy.79
  248.1 2.0 fusion.32
  250.2 1.9 fusion.17
  252.1 4.4 %copy.81 = f32[64,1024,16]{1,2,0:T(8,128)} copy(f32[64,1024,16]{1,0,2:T(8,128)S(1)} %fusion.17) | data formatting | bytes 8388608 | tf_op jit(solution)/shard_map/dsr,so->odr/dot_general | solution.py:156
  256.5 39.0 %all-to-all-done.5 = f32[64,16,512]{2,1,0:T(8,128)S(1)} async-done(((f32[64,16,512]{2,1,0:T(8,128)}), f32[64,16,512]{2,1,0:T(8,128)S(1)}, u32[]{:S(2)}, u32[]{:S(2)}) %all-to-all-start.5) | async-done | bytes 2097184 | tf_op jit(solution)/shard_map/all_to_all | solution.py:163
  295.5 6.0 %all-to-all-start.3 = ((f32[64,1024,16]{1,2,0:T(8,128)}), f32[64,1024,16]{1,2,0:T(8,128)}, u32[]{:S(2)}, u32[]{:S(2)}) async-start(f32[64,1024,16]{1,2,0:T(8,128)} %copy.81), calls=%async_computation.3 | async-start | bytes 8388608 | tf_op jit(solution)/shard_map/all_to_all | solution.py:155
  302.2 95.1 %all-to-all-done.3 = f32[64,1024,16]{1,2,0:T(8,128)} async-done(((f32[64,1024,16]{1,2,0:T(8,128)}), f32[64,1024,16]{1,2,0:T(8,128)}, u32[]{:S(2)}, u32[]{:S(2)}) %all-to-all-start.3) | async-done | bytes 4194336 | tf_op jit(solution)/shard_map/all_to_all | solution.py:155
  397.4 2.4 reduce_sum.66
  (120 shorter events, 39.6 us)
Async XLA Ops:
  7.2 100.7 %all-gather.4.cloned.1.call-start = ((), (), s32[]{:S(2)}) async-start(), calls=%async_computation.6 | async-start | bytes 1179648 | tf_op jit(solution)/shard_map/all_gather | solution.py:72
  9.2 17.7 %all-to-all-start.4 = ((bf16[128,8,16]{0,2,1:T(8,128)(2,1)}), bf16[128,8,16]{0,2,1:T(8,128)(2,1)S(1)}, u32[]{:S(2)}, u32[]{:S(2)}) async-start(bf16[128,8,16]{0,2,1:T(8,128)(2,1)} %tile.2), calls=%async_computation.4 | async-start | bytes 65536 | tf_op jit(solution)/shard_map/all_to_all | solution.py:86
  20.1 11.2 %copy-start.1 = (bf16[128,4096]{1,0:T(8,128)(2,1)S(1)}, bf16[128,4096]{1,0:T(8,128)(2,1)}, u32[]{:S(2)}) copy-start(bf16[128,4096]{1,0:T(8,128)(2,1)} %param.17) | copy-start | bytes 3145732
  26.9 39.3 %all-to-all-start = ((bf16[128,8,512]{0,2,1:T(8,128)(2,1)}), bf16[128,8,512]{0,2,1:T(8,128)(2,1)S(1)}, u32[]{:S(2)}, u32[]{:S(2)}) async-start(bf16[128,8,512]{0,2,1:T(8,128)(2,1)} %bitcast.9), calls=%async_computation | async-start | bytes 2097152 | tf_op jit(solution)/shard_map/all_to_all | solution.py:68
  30.5 81.1 %all-gather.6.cloned.1.call-start = ((), (), s32[]{:S(2)}) async-start(), calls=%async_computation.7 | async-start | bytes 1179648 | tf_op jit(solution)/shard_map/all_gather | solution.py:73
  31.3 39.3 %copy-start.8 = (s32[1,8]{1,0:T(1,128)S(1)}, s32[1,8]{1,0:T(1,128)}, u32[]{:S(2)}) copy-start(s32[1,8]{1,0:T(1,128)} %param.21) | copy-start | bytes 100
  66.2 35.3 %all-to-all-start.1 = ((bf16[128,8,512]{0,2,1:T(8,128)(2,1)}), bf16[128,8,512]{0,2,1:T(8,128)(2,1)S(1)}, u32[]{:S(2)}, u32[]{:S(2)}) async-start(bf16[128,8,512]{0,2,1:T(8,128)(2,1)} %bitcast.12), calls=%async_computation.1 | async-start | bytes 2097152 | tf_op jit(solution)/shard_map/all_to_all | solution.py:69
  69.8 129.6 %all-gather.8.cloned.1.call-start = ((), (), s32[]{:S(2)}) async-start(), calls=%async_computation.8 | async-start | bytes 1064960 | tf_op jit(solution)/shard_map/all_gather | solution.py:123
  70.8 4.2 %copy-start.6 = (s32[1,8]{1,0:T(1,128)S(1)}, s32[1,8]{1,0:T(1,128)}, u32[]{:S(2)}) copy-start(s32[1,8]{1,0:T(1,128)} %param.22) | copy-start | bytes 100
  70.8 4.2 %copy-start.9 = (s32[64]{0:T(128)S(1)}, s32[64]{0:T(128)}, u32[]{:S(2)}) copy-start(s32[64]{0:T(128)} %param.23) | copy-start | bytes 772
  101.5 128.7 %all-to-all-start.2 = ((bf16[128,8,1024]{0,2,1:T(8,128)(2,1)}), bf16[128,8,1024]{0,2,1:T(8,128)(2,1)}, u32[]{:S(2)}, u32[]{:S(2)}) async-start(bf16[128,8,1024]{0,2,1:T(8,128)(2,1)} %bitcast.20), calls=%async_computation.2 | async-start | bytes 4194304 | tf_op jit(solution)/shard_map/all_to_all | solution.py:85
  172.4 28.9 %copy-start.7 = (s32[1,8]{1,0:T(1,128)S(1)}, s32[1,8]{1,0:T(1,128)}, u32[]{:S(2)}) copy-start(s32[1,8]{1,0:T(1,128)} %param.22) | copy-start | bytes 100
  172.4 29.2 %copy-start = (bf16[4,1024,128]{1,2,0:T(8,128)(2,1)S(1)}, bf16[4,1024,128]{1,2,0:T(8,128)(2,1)}, u32[]{:S(2)}) copy-start(bf16[4,1024,128]{1,2,0:T(8,128)(2,1)} %get-tuple-element.86) | copy-start | bytes 3145732
  172.4 29.2 %copy-start.4 = (f32[1024,8]{0,1:T(8,128)S(1)}, f32[1024,8]{0,1:T(8,128)}, u32[]{:S(2)}) copy-start(f32[1024,8]{0,1:T(8,128)} %get-tuple-element.181) | copy-start | bytes 98308
  201.6 24.5 %copy-start.2 = (bf16[1024,16]{0,1:T(8,128)(2,1)S(1)}, bf16[1024,16]{0,1:T(8,128)(2,1)}, u32[]{:S(2)}) copy-start(bf16[1024,16]{0,1:T(8,128)(2,1)} %copy_bitcast_fusion) | copy-start | bytes 98308
  201.6 24.5 %copy-start.3 = (bf16[1024,8]{0,1:T(8,128)(2,1)S(1)}, bf16[1024,8]{0,1:T(8,128)(2,1)}, u32[]{:S(2)}) copy-start(bf16[1024,8]{0,1:T(8,128)(2,1)} %get-tuple-element.180) | copy-start | bytes 49156
  201.9 24.7 %copy-start.5 = (s32[8]{0:T(128)S(1)}, s32[8]{0:T(128)}, u32[]{:S(2)}) copy-start(s32[8]{0:T(128)} %select_reduce_fusion) | copy-start | bytes 100
  230.2 65.2 %all-to-all-start.5 = ((f32[64,16,512]{2,1,0:T(8,128)}), f32[64,16,512]{2,1,0:T(8,128)S(1)}, u32[]{:S(2)}, u32[]{:S(2)}) async-start(f32[64,16,512]{2,1,0:T(8,128)} %copy.85), calls=%async_computation.5 | async-start | bytes 4194304 | tf_op jit(solution)/shard_map/all_to_all | solution.py:163
  295.5 101.9 %all-to-all-start.3 = ((f32[64,1024,16]{1,2,0:T(8,128)}), f32[64,1024,16]{1,2,0:T(8,128)}, u32[]{:S(2)}, u32[]{:S(2)}) async-start(f32[64,1024,16]{1,2,0:T(8,128)} %copy.81), calls=%async_computation.3 | async-start | bytes 8388608 | tf_op jit(solution)/shard_map/all_to_all | solution.py:155
Sparse Core Ops, SparseCore 0:
  10.1 55.7 all-gather.3
  67.9 43.5 all-gather.5
  114.9 84.4 all-gather.7
where the time goes:
time: 408 us; the launch traced here: 407 us
  waiting for transfers between devices  227 us (56%)
  local copies, waits for them, and re-layouts  43.6 us (11%)
  starting transfers between devices  42.4 us (10%)
  matrix products  24.2 us (6%)
  blocking collectives  24.1 us (6%)
  loops' own time  16.8 us (4%)
  other arithmetic  15 us (4%)
  between operations  14 us (3%)
    all_to_all x1, waiting for transfers between devices, on_device(): lax.all_to_all(jnp.einsum('dsr,so->odr', part_a, slot_cols, precision=HIG...  95.1 us
    all_to_all x1, waiting for transfers between devices, on_device(): lax.all_to_all(jnp.einsum('srf,so->orf', part_b, slot_cols, precision=HIG...  39 us
    all_to_all x1, waiting for transfers between devices, on_device(): lax.all_to_all(queries, 'head', split_axis=1, concat_axis=0, tiled=True)  33.6 us
    all_gather x1, waiting for transfers between devices, on_device(): lax.all_gather(adapter_up_weight, 'seq', axis=0, tiled=True)  27 us
    psum x1, blocking collectives, on_device(): rank_low = lax.psum(rank_part, 'head').astype(jnp.bfloat16)  24.1 us
    all_to_all x1, waiting for transfers between devices, on_device(): lax.all_to_all(output_gradient, 'head', split_axis=1, concat_axis=0, tile...  22.7 us
    another operation x4, loops' own time, head_backward(): return lax.map(one_block, starts).reshape(pack_len, head_width)  16.5 us
    all_to_all x1, starting transfers between devices, on_device(): lax.all_to_all(jnp.einsum('srf,so->orf', part_b, slot_cols, precision=HIG...  14 us
  transfers between devices with their start and end apart: 9, of which 7 were waited for; matrix products, arithmetic and copies ran while one was open for 20% of the time, Pallas kernels for 0%

commit v1 on v0

v1 whole, which is shorter than its diff:
```python
import functools

import jax
import jax.numpy as jnp
from jax import lax
from jax.experimental import pallas as pl
from jax.experimental.pallas import tpu as pltpu
from jax.sharding import PartitionSpec as P

MESH = pl.DeviceIdType.MESH
F32, BF16, I32 = jnp.float32, jnp.bfloat16, jnp.int32

NX, NY, NZ = 4, 8, 8
HEAD_SIZE = 128
KV_HEADS = 4
GROUP = 8
RANK = 16
SEGMENTS = 8
COLS = SEGMENTS * RANK
TOKENS = 128
HALO = 3
KEYS = (HALO + 1) * TOKENS
WIDTH = 512
ADAPTER_SCALE = 2.0
SCORE_SCALE = 1.0 / HEAD_SIZE**0.5


def nt(a, b):
    return lax.dot_general(a, b, (((1,), (1,)), ((), ())), preferred_element_type=F32)


def nn(a, b):
    return lax.dot_general(a, b, (((1,), (0,)), ((), ())), preferred_element_type=F32)


class RingSum:
    def __init__(self, size, me, peer, chunk, sent, landed, send_sem, recv_sem, right):
        self.size, self.me, self.peer, self.chunk = size, me, peer, chunk
        self.sent, self.landed = sent, landed
        self.send_sem, self.recv_sem = send_sem, recv_sem
        self.ways = ((1, right, 0), (-1, size - 1 - right, right))
        self.copies = {}

    def stage(self, step):
        for sign, hops, base in self.ways:
            if step >= hops:
                continue
            slot = base + step
            target = lax.rem(self.me + sign * (hops - step) + self.size, self.size)
            total = self.chunk(target)
            if step > 0:
                self.copies[slot - 1].wait_recv()
                total = total + self.landed(slot - 1)[...].astype(F32)
            self.sent(slot)[...] = total.astype(self.sent(slot).dtype)
            copy = pltpu.make_async_remote_copy(
                src_ref=self.sent(slot),
                dst_ref=self.landed(slot),
                send_sem=self.send_sem(slot),
                recv_sem=self.recv_sem(slot),
                device_id=self.peer(sign),
                device_id_type=MESH,
            )
            copy.start()
            self.copies[slot] = copy

    def final(self):
        total = self.chunk(self.me)
        for _, hops, base in self.ways:
            slot = base + hops - 1
            self.copies[slot].wait_recv()
            total = total + self.landed(slot)[...].astype(F32)
        return total

    def drain(self):
        for copy in self.copies.values():
            copy.wait_send()


def kernel(
    q_hbm,
    g_hbm,
    x_hbm,
    k_ref,
    v_ref,
    act_ref,
    w_ref,
    len_ref,
    ada_ref,
    own_ref,
    down_ref,
    up_ref,
    qv,
    gv,
    xv,
    kb,
    vb,
    bias,
    dq,
    wall,
    wz,
    act_cols,
    rank_cols,
    slots,
    meta_s,
    meta_r,
    zs,
    zr,
    eb,
    ys,
    yr,
    xs,
    xr,
    xs2,
    xr2,
    ys2,
    yr2,
    ty,
    tx,
    load_sem,
    kv_send,
    kv_recv,
    wy_send,
    wy_recv,
    wx_send,
    wx_recv,
    wc_send,
    wc_recv,
    wz_send,
    wz_recv,
    zr_send,
    zr_recv,
    e_send,
    e_recv,
    f_send,
    f_recv,
    s_send,
    s_recv,
    m_send,
    m_recv,
):
    s = lax.axis_index("seq")
    z = lax.axis_index("head")
    core = lax.rem(s, 2)
    y = lax.rem(s // 2, NY)
    x = s // (2 * NY)

    def at_z(d):
        return (s, lax.rem(z + d + NZ, NZ))

    def at_y(d):
        return (x * (2 * NY) + lax.rem(y + d + NY, NY) * 2 + core, z)

    def at_x(d):
        return (lax.rem(x + d + NX, NX) * (2 * NY) + y * 2 + core, z)

    partner = (s + 1 - 2 * core, z)

    loads = []
    for g in range(KV_HEADS):
        lanes = pl.ds(g * GROUP * HEAD_SIZE, GROUP * HEAD_SIZE)
        for i, (src, dst) in enumerate(((q_hbm, qv), (g_hbm, gv))):
            copy = pltpu.make_async_copy(src.at[:, lanes], dst.at[:, lanes], load_sem.at[2 * g + i])
            copy.start()
            loads.append(copy)
    x_load = pltpu.make_async_copy(x_hbm, xv, load_sem.at[2 * KV_HEADS])
    x_load.start()

    barrier = pltpu.get_barrier_semaphore()
    others = (
        [at_z(d) for d in (1, 2, 3, -1, -2, -3)]
        + [at_y(d) for d in range(1, NY)]
        + [at_x(d) for d in range(1, NX)]
        + [partner]
    )
    for other in others:
        pl.semaphore_signal(barrier, inc=1, device_id=other, device_id_type=MESH)
    pl.semaphore_wait(barrier, len(others))

    def remote(src, dst, send, recv, to):
        copy = pltpu.make_async_remote_copy(
            src_ref=src, dst_ref=dst, send_sem=send, recv_sem=recv, device_id=to, device_id_type=MESH
        )
        copy.start()
        return copy

    sends = []
    kv_copies = []
    for g in range(KV_HEADS):
        lanes = pl.ds(g * HEAD_SIZE, HEAD_SIZE)
        row = []
        for d in range(1, HALO + 1):
            rows = pl.ds((HALO - d) * TOKENS, TOKENS)
            for i, (src, dst) in enumerate(((k_ref, kb), (v_ref, vb))):
                at = (g * HALO + d - 1) * 2 + i
                row.append(
                    remote(src.at[:, lanes], dst.at[rows, lanes], kv_send.at[at], kv_recv.at[at], at_z(d))
                )
        kv_copies.append(row)
        sends += row

    place = core * (NX * NY) + x * NY + y
    wy = []
    for d in range(1, NY):
        wy.append(remote(w_ref.at[0], wall.at[place], wy_send.at[d], wy_recv.at[d], at_y(d)))
    sends += wy
    wall[place] = w_ref[0]

    ends, total = [], 0
    for i in range(SEGMENTS):
        total = total + len_ref[0, i]
        ends.append(total)
    starts = [0] + ends[:-1]
    lane = lax.broadcasted_iota(I32, (8, COLS), 1)
    slot = lax.rem(lane, RANK)
    for i in range(SEGMENTS):
        owner = own_ref[ada_ref[0, i]]
        slot = slot + jnp.where(lane // RANK == i, owner * RANK, 0)
    meta_s[...] = slot
    slots[:, 0:COLS] = slot
    meta = remote(meta_s, meta_r, m_send.at[0], m_recv.at[0], partner)
    sends.append(meta)

    kb[HALO * TOKENS : KEYS, :] = k_ref[...]
    vb[HALO * TOKENS : KEYS, :] = v_ref[...]

    first = z * TOKENS
    row_pos = first + lax.broadcasted_iota(I32, (TOKENS, 1), 0)
    row_start = jnp.zeros((TOKENS, 1), I32)
    for i in range(1, SEGMENTS):
        row_start = jnp.where(row_pos >= starts[i], starts[i], row_start)
    key_pos = first - HALO * TOKENS + lax.broadcasted_iota(I32, (TOKENS, KEYS), 1)
    allowed = (key_pos >= row_start) & (key_pos <= row_pos)
    bias[...] = jnp.where(allowed, 0.0, -1e30).astype(F32)

    col = lax.broadcasted_iota(I32, (COLS, 1), 0)
    col_start = jnp.zeros((COLS, 1), I32)
    col_end = jnp.zeros((COLS, 1), I32)
    col_row = lax.rem(col, RANK)
    for i in range(SEGMENTS):
        here = col // RANK == i
        col_start = jnp.where(here, starts[i], col_start)
        col_end = jnp.where(here, ends[i], col_end)
        adapter = ada_ref[0, i]
        adapter_row = (lax.rem(adapter, 2) * (NX * NY) + adapter // 2) * RANK
        col_row = col_row + jnp.where(here, adapter_row, 0)
    token = first + lax.broadcasted_iota(I32, (COLS, TOKENS), 1)
    mask = (token >= col_start) & (token < col_end)
    spread = lax.rem(lax.broadcasted_iota(I32, (COLS, RANK), 0), RANK) == lax.broadcasted_iota(
        I32, (COLS, RANK), 1
    )
    spread = jnp.where(spread, 1.0, 0.0).astype(BF16)
    act_cols[...] = jnp.where(mask, nn(spread, act_ref[...]), 0.0).astype(BF16)

    def attend(g):
        for i in range(2):
            loads[2 * g + i].wait()
        for copy in kv_copies[g]:
            copy.wait_recv()
        lanes = pl.ds(g * HEAD_SIZE, HEAD_SIZE)

        def head(h, carry):
            at = pl.ds(pl.multiple_of((g * GROUP + h) * HEAD_SIZE, HEAD_SIZE), HEAD_SIZE)
            keys, values = kb[:, lanes], vb[:, lanes]
            scores = nt(qv[:, at], keys) * SCORE_SCALE + bias[...]
            weights = jnp.exp(scores - jnp.max(scores, axis=1, keepdims=True))
            scale = 1.0 / jnp.sum(weights, axis=1, keepdims=True)
            d_prob = nt(gv[:, at], values)
            delta = jnp.sum(weights * d_prob, axis=1, keepdims=True) * scale
            dscore = (weights * (d_prob - delta) * (scale * SCORE_SCALE)).astype(BF16)
            dq[:, at] = nn(dscore, keys).astype(BF16)
            return carry

        lax.fori_loop(0, GROUP, head, 0, unroll=2)

    for copy in wy:
        copy.wait_recv()
    mine = core * (NX * NY)

    def block(d):
        return wall.at[pl.ds(mine + lax.rem(x - d + NX, NX) * NY, NY)]

    wx = [None]
    for d in range(1, NX):
        wx.append(remote(block(0), block(0), wx_send.at[d], wx_recv.at[d], at_x(d)))
    wc = [remote(block(0), block(0), wc_send.at[0], wc_recv.at[0], partner)]
    sends += wx[1:]

    attend(0)
    for d in range(1, NX):
        wx[d].wait_recv()
        wc.append(remote(block(d), block(d), wc_send.at[d], wc_recv.at[d], partner))
    sends += wc
    attend(1)

    for copy in wc:
        copy.wait_recv()
    pick = jnp.where(lax.broadcasted_iota(I32, (COLS, 2 * NX * NY * RANK), 1) == col_row, 1.0, 0.0)
    wz[z] = nn(pick.astype(BF16), wall[...].reshape(2 * NX * NY * RANK, WIDTH)).astype(BF16)
    wz_ways = ((1, 3, 0), (-1, 4, 3))
    wz_copies = {}

    def pass_on(step):
        for sign, hops, base in wz_ways:
            if step < hops:
                if step > 0:
                    wz_copies[base + step - 1].wait_recv()
                at = lax.rem(z - sign * step + NZ, NZ)
                wz_copies[base + step] = remote(
                    wz.at[at], wz.at[at], wz_send.at[base + step], wz_recv.at[base + step], at_z(sign)
                )

    pass_on(0)
    attend(2)
    pass_on(1)
    attend(3)
    pass_on(2)

    def part(c, rows):
        return nt(wz[rows], dq[:, pl.ds(pl.multiple_of(c * WIDTH, WIDTH), WIDTH)])

    def b_chunk(c):
        return nn(act_cols[...], dq[:, pl.ds(pl.multiple_of(c * WIDTH, WIDTH), WIDTH)])

    def a_chunk(j, c):
        return nn(rank_cols[...], xv[:, pl.ds(pl.multiple_of((2 * c + j) * WIDTH, WIDTH), WIDTH)])

    def z_sum(blk, chunk, right):
        return RingSum(
            NZ,
            z,
            at_z,
            chunk,
            lambda i: zs.at[blk, i],
            lambda i: zr.at[blk, i],
            lambda i: zr_send.at[blk, i],
            lambda i: zr_recv.at[blk, i],
            right,
        )

    zsum = [
        z_sum(0, b_chunk, 3),
        z_sum(1, functools.partial(a_chunk, 0), 4),
        z_sum(2, functools.partial(a_chunk, 1), 4),
    ]
    zsum[0].stage(0)
    pass_on(3)
    for i in (2, 6):
        wz_copies[i].wait_recv()
    sends += list(wz_copies.values())
    rank = part(0, 0)
    for c in range(1, NZ):
        rank = rank + part(c, c)
    rank_cols[...] = jnp.where(mask, rank, 0.0).astype(BF16)
    x_load.wait()

    e_copies = {}

    def to_partner(blk):
        eb[blk, 0:COLS] = zsum[blk].final().astype(BF16)
        e_copies[blk] = remote(
            eb.at[blk, pl.ds(0, COLS)],
            eb.at[blk, pl.ds(COLS, COLS)],
            e_send.at[blk],
            e_recv.at[blk],
            partner,
        )

    def y_chunk(blk, c):
        row = lax.broadcasted_iota(I32, (NX * RANK, 2 * COLS), 0)
        key = (row // RANK) * (2 * NY * RANK) + (c * 2 + core) * RANK + lax.rem(row, RANK)
        return nn(jnp.where(key == slots[0:1, :], 1.0, 0.0).astype(BF16), eb[blk])

    def x_chunk(blk, c):
        row = lax.broadcasted_iota(I32, (NY * RANK, 2 * COLS), 0)
        key = (c * 2 * NY + (row // RANK) * 2 + core) * RANK + lax.rem(row, RANK)
        return nn(jnp.where(key == slots[0:1, :], 1.0, 0.0).astype(BF16), eb[blk])

    def rows_of(buf, c):
        return buf[pl.ds(pl.multiple_of(c * RANK, RANK), RANK), :]

    def f_sems(blk):
        return (lambda i: f_send.at[blk, i]), (lambda i: f_recv.at[blk, i])

    def s_sems(blk):
        return (lambda i: s_send.at[blk, i]), (lambda i: s_recv.at[blk, i])

    def y_first(blk, at):
        one = RingSum(
            NY, y, at_y, functools.partial(y_chunk, blk),
            lambda i: ys.at[at, i], lambda i: yr.at[at, i], *f_sems(blk), 4,
        )
        two = RingSum(
            NX, x, at_x, lambda c: rows_of(ty.at[at], c),
            lambda i: xs2.at[at, i], lambda i: xr2.at[at, i], *s_sems(blk), 2,
        )
        return one, two, ty.at[at]

    def x_first(blk, at):
        one = RingSum(
            NX, x, at_x, functools.partial(x_chunk, blk),
            lambda i: xs.at[at, i], lambda i: xr.at[at, i], *f_sems(blk), 2,
        )
        two = RingSum(
            NY, y, at_y, lambda c: rows_of(tx.at[at], c),
            lambda i: ys2.at[at, i], lambda i: yr2.at[at, i], *s_sems(blk), 4,
        )
        return one, two, tx.at[at]

    seq_sum = [y_first(0, 0), x_first(1, 0), y_first(2, 1)]
    outs = [
        (up_ref, pl.ds(0, WIDTH)),
        (down_ref, pl.ds(0, WIDTH)),
        (down_ref, pl.ds(WIDTH, WIDTH)),
    ]

    for step in range(4):
        for blk in (0, 1, 2):
            if blk > 0 or step > 0:
                zsum[blk].stage(step)
    meta.wait_recv()
    slots[:, COLS : 2 * COLS] = meta_r[...]
    for blk in (0, 1, 2):
        to_partner(blk)
    for step in range(4):
        for blk in (0, 1, 2):
            if step == 0:
                e_copies[blk].wait_recv()
            one = seq_sum[blk][0]
            if step < one.ways[0][1]:
                one.stage(step)
    for blk in (1, 0, 2):
        one, two, held = seq_sum[blk]
        held[...] = one.final()
        two.stage(0)
    for step in range(1, 4):
        for blk in (1, 0, 2):
            two = seq_sum[blk][1]
            if step < two.ways[0][1]:
                two.stage(step)
    for blk in (0, 2, 1):
        ref, lanes = outs[blk]
        ref[:, lanes] = seq_sum[blk][1].final() * ADAPTER_SCALE

    for copy in sends + list(e_copies.values()):
        copy.wait_send()
    for ring in zsum:
        ring.drain()
    for one, two, _ in seq_sum:
        one.drain()
        two.drain()


def on_device(q, k, v, g, x, act, w, length, adapter, owner):
    vmem = pl.BlockSpec(memory_space=pltpu.VMEM)
    smem = pl.BlockSpec(memory_space=pltpu.SMEM)
    hbm = pl.BlockSpec(memory_space=pl.ANY)
    dma = pltpu.SemaphoreType.DMA
    ring = NZ - 1
    scratch = [
        pltpu.VMEM((TOKENS, KV_HEADS * GROUP * HEAD_SIZE), BF16),
        pltpu.VMEM((TOKENS, KV_HEADS * GROUP * HEAD_SIZE), BF16),
        pltpu.VMEM((TOKENS, x.shape[1]), BF16),
        pltpu.VMEM((KEYS, WIDTH), BF16),
        pltpu.VMEM((KEYS, WIDTH), BF16),
        pltpu.VMEM((TOKENS, KEYS), F32),
        pltpu.VMEM((TOKENS, KV_HEADS * GROUP * HEAD_SIZE), BF16),
        pltpu.VMEM((2 * NX * NY, RANK, WIDTH), BF16),
        pltpu.VMEM((NZ, COLS, WIDTH), BF16),
        pltpu.VMEM((COLS, TOKENS), BF16),
        pltpu.VMEM((COLS, TOKENS), BF16),
        pltpu.VMEM((8, 2 * COLS), I32),
        pltpu.VMEM((8, COLS), I32),
        pltpu.VMEM((8, COLS), I32),
        pltpu.VMEM((3, ring, COLS, WIDTH), BF16),
        pltpu.VMEM((3, ring, COLS, WIDTH), BF16),
        pltpu.VMEM((3, 2 * COLS, WIDTH), BF16),
        pltpu.VMEM((2, NY - 1, NX * RANK, WIDTH), BF16),
        pltpu.VMEM((2, NY - 1, NX * RANK, WIDTH), BF16),
        pltpu.VMEM((1, NX - 1, NY * RANK, WIDTH), BF16),
        pltpu.VMEM((1, NX - 1, NY * RANK, WIDTH), BF16),
        pltpu.VMEM((2, NX - 1, RANK, WIDTH), F32),
        pltpu.VMEM((2, NX - 1, RANK, WIDTH), F32),
        pltpu.VMEM((1, NY - 1, RANK, WIDTH), F32),
        pltpu.VMEM((1, NY - 1, RANK, WIDTH), F32),
        pltpu.VMEM((2, NX * RANK, WIDTH), F32),
        pltpu.VMEM((1, NY * RANK, WIDTH), F32),
        dma((2 * KV_HEADS + 1,)),
        dma((KV_HEADS * HALO * 2,)),
        dma((KV_HEADS * HALO * 2,)),
        dma((NY,)),
        dma((NY,)),
        dma((NX,)),
        dma((NX,)),
        dma((NX,)),
        dma((NX,)),
        dma((ring,)),
        dma((ring,)),
        dma((3, ring)),
        dma((3, ring)),
        dma((3,)),
        dma((3,)),
        dma((3, ring)),
        dma((3, ring)),
        dma((3, ring)),
        dma((3, ring)),
        dma((1,)),
        dma((1,)),
    ]
    down, up = pl.pallas_call(
        kernel,
        out_shape=(
            jax.ShapeDtypeStruct((RANK, 2 * WIDTH), F32),
            jax.ShapeDtypeStruct((RANK, WIDTH), F32),
        ),
        in_specs=[hbm, hbm, hbm, vmem, vmem, vmem, vmem, smem, smem, smem],
        out_specs=(vmem, vmem),
        scratch_shapes=scratch,
        compiler_params=pltpu.CompilerParams(
            collective_id=0, has_side_effects=True, vmem_limit_bytes=40 * 1024 * 1024
        ),
    )(q, g, x, k, v, act.T, w, length, adapter, owner)
    return down.T[None], up[None]


def solution(mesh):
    return jax.shard_map(
        on_device,
        mesh=mesh,
        in_specs=(
            P(("seq", "head"), None),
            P(("seq", "head"), None),
            P(("seq", "head"), None),
            P(("seq", "head"), None),
            P(("seq", "head"), None),
            P(("seq", "head"), None),
            P("seq", None, "head"),
            P("seq", None),
            P("seq", None),
            P(),
        ),
        out_specs=(P("seq", "head", None), P("seq", None, "head")),
        check_vma=False,
    )
```

time: 408 us -> 138 us (0.34)
  the two profiles are of different devices: /device:TPU:1 before, /device:TPU:64 now
where the time goes in v1:
time: 138 us; the launch traced here: 137 us
  Pallas kernels  126 us (91%)
  local copies, waits for them, and re-layouts  10.5 us (8%)
    pallas_call x1, Pallas kernels, on_device(): pl.pallas_call(kernel, out_shape=(jax.ShapeDtypeStruct((RANK, 2 * WIDTH),...  126 us
    unnamed x22, local copies, waits for them, and re-layouts  10.5 us

profile of v1, /device:TPU:64, one launch (start us, length us, event | category | flops | bytes accessed | tf_op | source)
XLA Modules:
  0.0 137.5 jit_solution(10083495217509622804)
XLA Ops:
  0.6 0.0 copy-start
  0.6 1.6 %copy-done = bf16[128,8192]{1,0:T(8,128)(2,1)S(1)} copy-done((bf16[128,8192]{1,0:T(8,128)(2,1)S(1)}, bf16[128,8192]{1,0:T(8,128)(2,1)}, u32[]{:S(2)}) %copy-start) | copy-done | bytes 2097176
  2.2 0.0 copy-start.1
  2.2 1.2 copy-done.1
  3.5 0.0 copy-start.2
  3.5 1.2 copy-done.2
  4.7 0.0 copy-start.3
  4.7 0.9 copy-done.3
  5.6 0.0 copy-start.4
  5.6 0.9 copy-done.4
  6.5 0.0 copy-start.5
  6.5 0.7 copy-done.5
  7.2 0.0 copy-start.6
  7.2 0.7 copy-done.6
  7.9 0.0 copy-start.7
  7.9 0.7 copy-done.7
  8.5 0.0 copy-start.8
  8.5 0.7 copy-done.8
  9.2 0.0 copy-start.9
  9.2 0.7 copy-done.9
  9.9 126.4 %shard_map.113 = (f32[16,1024]{1,0:T(8,128)S(1)}, f32[16,512]{1,0:T(8,128)S(1)}) custom-call(bf16[128,4096]{1,0:T(8,128)(2,1)S(1)} %copy-done.1, bf16[128,4096]{1,0:T(8,128)(2,1)S(1)} %copy-done.2, bf16[128,8192]{1,0:T(8,128)(2,1)S(1)} %copy-done, bf16[128,512]{1,0:T(8,128)(2,1)S(1)} %copy-done.3, bf16[128,512]{1,0:T(8,128)(2,1)S(1)} %copy-done.4, ...), custom_call_target="tpu_custom_call" | custom-call | tf_op jit(solution)/shard_map/pallas_call | solution.py:509
  136.2 0.6 copy.14
  136.9 0.6 copy.15
Async XLA Ops:
  0.6 1.6 %copy-start = (bf16[128,8192]{1,0:T(8,128)(2,1)S(1)}, bf16[128,8192]{1,0:T(8,128)(2,1)}, u32[]{:S(2)}) copy-start(bf16[128,8192]{1,0:T(8,128)(2,1)} %x_hbm.1) | copy-start | bytes 6291460
  2.2 1.2 copy-start.1
  3.5 1.2 copy-start.2
  4.7 0.9 copy-start.3
  5.6 0.9 copy-start.4
  6.5 0.7 copy-start.5
  7.2 0.7 copy-start.6
  7.9 0.7 copy-start.7
  8.5 0.7 copy-start.8
  9.2 0.7 copy-start.9

commit v2 on v1

v2 whole, which is shorter than its diff:
```python
import functools

import jax
import jax.numpy as jnp
from jax import lax
from jax.experimental import pallas as pl
from jax.experimental.pallas import tpu as pltpu
from jax.sharding import PartitionSpec as P

MESH = pl.DeviceIdType.MESH
F32, BF16, I32 = jnp.float32, jnp.bfloat16, jnp.int32

NX, NY, NZ = 4, 8, 8
HEAD_SIZE = 128
KV_HEADS = 4
GROUP = 8
RANK = 16
PAIR = 2
SEGMENTS = 8
COLS = SEGMENTS * RANK
TOKENS = 128
HALO = 3
KEYS = (HALO + 1) * TOKENS
WIDTH = 512
PIECE = 256
PIECES = 6
BEGIN = (-1, -1, 0, 0, 0, 0)
Y_FIRST = (0, 2)
ADAPTER_SCALE = 2.0
SCORE_SCALE = 1.0 / HEAD_SIZE**0.5


def nt(a, b):
    return lax.dot_general(a, b, (((1,), (1,)), ((), ())), preferred_element_type=F32)


def nn(a, b):
    return lax.dot_general(a, b, (((1,), (0,)), ((), ())), preferred_element_type=F32)


class RingSum:
    def __init__(self, size, me, peer, chunk, sent, landed, send_sem, recv_sem, right):
        self.size, self.me, self.peer, self.chunk = size, me, peer, chunk
        self.sent, self.landed = sent, landed
        self.send_sem, self.recv_sem = send_sem, recv_sem
        self.ways = ((1, right, 0), (-1, size - 1 - right, right))
        self.copies = {}

    def stage(self, step):
        for sign, hops, base in self.ways:
            if step >= hops:
                continue
            slot = base + step
            target = lax.rem(self.me + sign * (hops - step) + self.size, self.size)
            total = self.chunk(target)
            if step > 0:
                self.copies[slot - 1].wait_recv()
                total = total + self.landed(slot - 1)[...].astype(F32)
            self.sent(slot)[...] = total.astype(self.sent(slot).dtype)
            copy = pltpu.make_async_remote_copy(
                src_ref=self.sent(slot),
                dst_ref=self.landed(slot),
                send_sem=self.send_sem(slot),
                recv_sem=self.recv_sem(slot),
                device_id=self.peer(sign),
                device_id_type=MESH,
            )
            copy.start()
            self.copies[slot] = copy

    def final(self):
        total = self.chunk(self.me)
        for _, hops, base in self.ways:
            slot = base + hops - 1
            self.copies[slot].wait_recv()
            total = total + self.landed(slot)[...].astype(F32)
        return total

    def drain(self):
        for copy in self.copies.values():
            copy.wait_send()


class DirectSum:
    def __init__(self, size, me, peer, chunk, sent, landed, send_sem, recv_sem):
        self.size, self.me, self.peer, self.chunk = size, me, peer, chunk
        self.sent, self.landed = sent, landed
        self.send_sem, self.recv_sem = send_sem, recv_sem
        self.copies = []

    def stage(self, step):
        for d in range(1, self.size):
            to = lax.rem(self.me + d, self.size)
            self.sent(d - 1)[...] = self.chunk(to).astype(self.sent(d - 1).dtype)
            copy = pltpu.make_async_remote_copy(
                src_ref=self.sent(d - 1),
                dst_ref=self.landed(d - 1),
                send_sem=self.send_sem(d - 1),
                recv_sem=self.recv_sem(d - 1),
                device_id=self.peer(d),
                device_id_type=MESH,
            )
            copy.start()
            self.copies.append(copy)

    def final(self):
        total = self.chunk(self.me)
        for d, copy in enumerate(self.copies):
            copy.wait_recv()
            total = total + self.landed(d)[...].astype(F32)
        return total

    def drain(self):
        for copy in self.copies:
            copy.wait_send()


def kernel(
    q_hbm,
    g_hbm,
    x_hbm,
    k_hbm,
    v_hbm,
    act_hbm,
    w_hbm,
    len_ref,
    ada_ref,
    own_ref,
    down_ref,
    up_ref,
    qv,
    gv,
    xv,
    kv,
    bias,
    dq,
    wall,
    wz,
    act_v,
    act_cols,
    rank_cols,
    slots,
    pick_y,
    pick_x,
    meta_s,
    meta_r,
    zs,
    zr,
    eb,
    fys,
    fyr,
    fxs,
    fxr,
    sxs,
    sxr,
    sys_,
    syr,
    ty,
    tx,
    load_sem,
    kv_sem,
    wy_sem,
    wx_sem,
    wc_sem,
    wz_sem,
    z_sem,
    e_sem,
    f_sem,
    s_sem,
    m_sem,
):
    s = lax.axis_index("seq")
    z = lax.axis_index("head")
    core = lax.rem(s, 2)
    y = lax.rem(s // 2, NY)
    x = s // (2 * NY)

    def at_z(d):
        return (s, lax.rem(z + d + NZ, NZ))

    def at_y(d):
        return (x * (2 * NY) + lax.rem(y + d + NY, NY) * 2 + core, z)

    def at_x(d):
        return (lax.rem(x + d + NX, NX) * (2 * NY) + y * 2 + core, z)

    partner = (s + 1 - 2 * core, z)

    barrier = pltpu.get_barrier_semaphore()
    others = (
        [at_z(1), at_z(-1), partner]
        + [at_y(d) for d in range(1, NY)]
        + [at_x(d) for d in range(1, NX)]
    )
    for other in others:
        pl.semaphore_signal(barrier, inc=1, device_id=other, device_id_type=MESH)

    places = (core * (NX * NY) + x * NY + y, core * (NX * NY) + y * NX + x)
    load_count = [0]

    def load(src, dst):
        copy = pltpu.make_async_copy(src, dst, load_sem.at[load_count[0]])
        load_count[0] += 1
        copy.start()
        return copy

    own_kv = []
    for g in range(KV_HEADS):
        lanes = pl.ds(g * HEAD_SIZE, HEAD_SIZE)
        own_kv.append([load(src.at[:, lanes], kv.at[HALO, g, i]) for i, src in enumerate((k_hbm, v_hbm))])
    w_load = [load(w_hbm.at[0, :, pl.ds(h * PIECE, PIECE)], wall.at[h, places[h]]) for h in range(2)]
    act_load = load(act_hbm, act_v)

    sends = []

    def remote(src, dst, sem, at, to):
        copy = pltpu.make_async_remote_copy(
            src_ref=src,
            dst_ref=dst,
            send_sem=sem.at[0, at],
            recv_sem=sem.at[1, at],
            device_id=to,
            device_id_type=MESH,
        )
        copy.start()
        sends.append(copy)
        return copy

    kv_copies = {}

    def send_kv(g, d):
        if d == 0:
            for copy in own_kv[g]:
                copy.wait()
        else:
            kv_copies[g, d].wait_recv()
        if d < HALO:
            kv_copies[g, d + 1] = remote(
                kv.at[HALO - d, g], kv.at[HALO - d - 1, g], kv_sem, g * HALO + d, at_z(1)
            )

    for copy in w_load:
        copy.wait()
    pl.semaphore_wait(barrier, len(others))

    def pass_w(h, rows, sem, at, to):
        return remote(wall.at[h, rows], wall.at[h, rows], sem, at, to)

    w_one = [
        [pass_w(0, places[0], wy_sem, d, at_y(d)) for d in range(1, NY)],
        [pass_w(1, places[1], wx_sem, d, at_x(d)) for d in range(1, NX)],
    ]
    for g in range(KV_HEADS):
        send_kv(g, 0)
    qg_load = []
    for g in range(KV_HEADS):
        lanes = pl.ds(g * GROUP * HEAD_SIZE, GROUP * HEAD_SIZE)
        qg_load.append([load(src.at[:, lanes], dst.at[:, lanes]) for src, dst in ((q_hbm, qv), (g_hbm, gv))])

    ends, total = [], 0
    for i in range(SEGMENTS):
        total = total + len_ref[0, i]
        ends.append(total)
    starts = [0] + ends[:-1]
    lane = lax.broadcasted_iota(I32, (8, COLS), 1)
    slot = lax.rem(lane, RANK)
    for i in range(SEGMENTS):
        owner = own_ref[ada_ref[0, i]]
        slot = slot + jnp.where(lane // RANK == i, owner * RANK, 0)
    meta_s[...] = slot
    slots[:, 0:COLS] = slot
    meta = remote(meta_s, meta_r, m_sem, 0, partner)

    first = z * TOKENS
    row_pos = first + lax.broadcasted_iota(I32, (TOKENS, 1), 0)
    row_start = jnp.zeros((TOKENS, 1), I32)
    for i in range(1, SEGMENTS):
        row_start = jnp.where(row_pos >= starts[i], starts[i], row_start)
    key_pos = first - HALO * TOKENS + lax.broadcasted_iota(I32, (TOKENS, KEYS), 1)
    allowed = (key_pos >= row_start) & (key_pos <= row_pos)
    bias[...] = jnp.where(allowed, 0.0, -1e30).astype(F32)

    col = lax.broadcasted_iota(I32, (COLS, 1), 0)
    col_start = jnp.zeros((COLS, 1), I32)
    col_end = jnp.zeros((COLS, 1), I32)
    col_rows = [lax.rem(col, RANK)] * 2
    for i in range(SEGMENTS):
        here = col // RANK == i
        col_start = jnp.where(here, starts[i], col_start)
        col_end = jnp.where(here, ends[i], col_end)
        adapter = ada_ref[0, i]
        chip = adapter // 2
        for h, at in enumerate((chip, lax.rem(chip, NY) * NX + chip // NY)):
            adapter_row = (lax.rem(adapter, 2) * (NX * NY) + at) * RANK
            col_rows[h] = col_rows[h] + jnp.where(here, adapter_row, 0)
    token = first + lax.broadcasted_iota(I32, (COLS, TOKENS), 1)
    mask = (token >= col_start) & (token < col_end)
    spread = lax.rem(lax.broadcasted_iota(I32, (COLS, RANK), 0), RANK) == lax.broadcasted_iota(
        I32, (COLS, RANK), 1
    )
    spread = jnp.where(spread, 1.0, 0.0).astype(BF16)
    act_load.wait()
    act_cols[...] = jnp.where(mask, nn(spread, act_v[...]), 0.0).astype(BF16)

    def attend(g):
        for copy in qg_load[g]:
            copy.wait()
        kv_copies[g, HALO].wait_recv()

        def heads(i, carry):
            at = [
                pl.ds(pl.multiple_of((g * GROUP + PAIR * i + j) * HEAD_SIZE, HEAD_SIZE), HEAD_SIZE)
                for j in range(PAIR)
            ]
            keys = kv[:, g, 0].reshape(KEYS, HEAD_SIZE)
            values = kv[:, g, 1].reshape(KEYS, HEAD_SIZE)
            q_rows = jnp.concatenate([qv[:, lanes] for lanes in at], axis=0)
            g_rows = jnp.concatenate([gv[:, lanes] for lanes in at], axis=0)
            hidden = jnp.concatenate([bias[...]] * PAIR, axis=0)
            scores = nt(q_rows, keys) * SCORE_SCALE + hidden
            weights = jnp.exp(scores - jnp.max(scores, axis=1, keepdims=True))
            scale = 1.0 / jnp.sum(weights, axis=1, keepdims=True)
            d_prob = nt(g_rows, values)
            delta = jnp.sum(weights * d_prob, axis=1, keepdims=True) * scale
            dscore = (weights * (d_prob - delta) * (scale * SCORE_SCALE)).astype(BF16)
            grads = nn(dscore, keys).astype(BF16)
            for j in range(PAIR):
                dq[:, at[j]] = grads[j * TOKENS : (j + 1) * TOKENS]
            return carry

        lax.fori_loop(0, GROUP // PAIR, heads, 0)

    mine = core * (NX * NY)
    for copy in w_one[1]:
        copy.wait_recv()
    row = pl.ds(mine + y * NX, NX)
    w_two = [None, [pass_w(1, row, wy_sem, NY + d, at_y(d)) for d in range(1, NY)]]
    for copy in w_one[0]:
        copy.wait_recv()
    row = pl.ds(mine + x * NY, NY)
    w_two[0] = [pass_w(0, row, wx_sem, NX + d, at_x(d)) for d in range(1, NX)]
    for g in range(KV_HEADS):
        send_kv(g, 1)
    w_core = []
    for h in range(2):
        for copy in w_two[h]:
            copy.wait_recv()
        w_core.append(pass_w(h, pl.ds(mine, NX * NY), wc_sem, h, partner))
    for g in range(KV_HEADS):
        send_kv(g, 2)
    x_load = load(x_hbm, xv)
    meta.wait_recv()
    slots[:, COLS : 2 * COLS] = meta_r[...]

    wz_ways = ((1, 3, 0), (-1, 4, 3))
    wz_copies = {}

    def pass_on(h, step):
        for sign, hops, base in wz_ways:
            if step <= hops:
                if step > 0:
                    wz_copies[h, base + step - 1].wait_recv()
                if step < hops:
                    at = lax.rem(z - sign * step + NZ, NZ)
                    wz_copies[h, base + step] = remote(
                        wz.at[at, h], wz.at[at, h], wz_sem, h * (NZ - 1) + base + step, at_z(sign)
                    )

    every = lax.broadcasted_iota(I32, (COLS, 2 * NX * NY * RANK), 1)
    for h in range(2):
        w_core[h].wait_recv()
        pick = jnp.where(every == col_rows[h], 1.0, 0.0).astype(BF16)
        wz[z, h] = nn(pick, wall[h].reshape(2 * NX * NY * RANK, PIECE)).astype(BF16)
        pass_on(h, 0)
    def fill(i, carry):
        row = i * (NX * RANK) + lax.broadcasted_iota(I32, (NX * RANK, 2 * COLS), 0)
        low = core * RANK + lax.rem(row, RANK)
        chip = row // RANK
        rows = pl.ds(pl.multiple_of(i * (NX * RANK), NX * RANK), NX * RANK)
        key = (lax.rem(chip, NX) * NY + chip // NX) * (2 * RANK) + low
        pick_y[rows, :] = jnp.where(key == slots[0:1, :], 1.0, 0.0).astype(BF16)
        pick_x[rows, :] = jnp.where(chip * (2 * RANK) + low == slots[0:1, :], 1.0, 0.0).astype(BF16)
        return carry

    lax.fori_loop(0, NY, fill, 0)
    for g in range(KV_HEADS):
        attend(g)
        if g < 3:
            for h in range(2):
                pass_on(h, g + 1)

    def zcols(ref, c, i, width):
        return ref[:, pl.ds(pl.multiple_of(c * width + i * PIECE, PIECE), PIECE)]

    def z_chunk(p, c):
        if p < 2:
            return nn(act_cols[...], zcols(dq, c, p, WIDTH))
        return nn(rank_cols[...], zcols(xv, c, p - 2, 2 * WIDTH))

    def y_chunk(p, c):
        rows = pl.ds(pl.multiple_of(c * (NX * RANK), NX * RANK), NX * RANK)
        return nn(pick_y[rows, :], eb[p])

    def x_chunk(p, c):
        rows = pl.ds(pl.multiple_of(c * (NY * RANK), NY * RANK), NY * RANK)
        return nn(pick_x[rows, :], eb[p])

    def rows_of(buf, c):
        return buf[pl.ds(pl.multiple_of(c * RANK, RANK), RANK), :]

    def refs(p, at, sent, landed, sem):
        return (
            lambda i: sent.at[at, i],
            lambda i: landed.at[at, i],
            lambda i: sem.at[0, p, i],
            lambda i: sem.at[1, p, i],
        )

    z_sums, f_sums, s_sums, held, e_copies = [], [], [], [], {}
    for p in range(PIECES):
        z_sums.append(
            RingSum(NZ, z, at_z, functools.partial(z_chunk, p), *refs(p, p, zs, zr, z_sem), 4 - p % 2)
        )
        at = sum((i in Y_FIRST) == (p in Y_FIRST) for i in range(p))
        if p in Y_FIRST:
            held.append(ty.at[at])
            f_sums.append(
                DirectSum(NY, y, at_y, functools.partial(y_chunk, p), *refs(p, at, fys, fyr, f_sem))
            )
            s_sums.append(
                DirectSum(NX, x, at_x, functools.partial(rows_of, ty.at[at]), *refs(p, at, sxs, sxr, s_sem))
            )
        else:
            held.append(tx.at[at])
            f_sums.append(
                RingSum(NX, x, at_x, functools.partial(x_chunk, p), *refs(p, at, fxs, fxr, f_sem), 1 + p % 2)
            )
            s_sums.append(
                DirectSum(NY, y, at_y, functools.partial(rows_of, tx.at[at]), *refs(p, at, sys_, syr, s_sem))
            )

    def to_partner(p):
        eb[p, 0:COLS] = z_sums[p].final().astype(BF16)
        e_copies[p] = remote(eb.at[p, pl.ds(0, COLS)], eb.at[p, pl.ds(COLS, COLS)], e_sem, p, partner)

    def first_hop(p):
        e_copies[p].wait_recv()
        f_sums[p].stage(0)

    def turn(p):
        held[p][...] = f_sums[p].final()
        s_sums[p].stage(0)

    def write(p):
        ref, at = (up_ref, p) if p < 2 else (down_ref, p - 2)
        ref[:, at * PIECE : (at + 1) * PIECE] = s_sums[p].final() * ADAPTER_SCALE

    def rank_all():
        for h in range(2):
            pass_on(h, 4)
        rank = jnp.zeros((COLS, TOKENS), F32)
        for c in range(NZ):
            for h in range(2):
                at = c * WIDTH + h * PIECE
                rank = rank + nt(wz[c, h], dq[:, at : at + PIECE])
        rank_cols[...] = jnp.where(mask, rank, 0.0).astype(BF16)
        x_load.wait()

    plan = []
    for p, begin in enumerate(BEGIN):
        steps = [functools.partial(z_sums[p].stage, i) for i in range(4)]
        steps += [functools.partial(to_partner, p), functools.partial(first_hop, p)]
        if p not in Y_FIRST:
            steps.append(functools.partial(f_sums[p].stage, 1))
        steps += [functools.partial(turn, p), functools.partial(write, p)]
        plan += [(begin + i, 0 if i < 5 else 1, p, step) for i, step in enumerate(steps)]
    plan.append((0, -1, 0, rank_all))
    for _, _, _, step in sorted(plan, key=lambda entry: entry[:3]):
        step()

    for copy in sends:
        copy.wait_send()
    for sums in z_sums + f_sums + s_sums:
        sums.drain()


def on_device(q, k, v, g, x, act, w, length, adapter, owner):
    vmem = pl.BlockSpec(memory_space=pltpu.VMEM)
    smem = pl.BlockSpec(memory_space=pltpu.SMEM)
    hbm = pl.BlockSpec(memory_space=pl.ANY)
    dma = pltpu.SemaphoreType.DMA
    ring = NZ - 1
    by_y = len(Y_FIRST)
    by_x = PIECES - by_y
    features = KV_HEADS * GROUP * HEAD_SIZE
    scratch = [
        pltpu.VMEM((TOKENS, features), BF16),
        pltpu.VMEM((TOKENS, features), BF16),
        pltpu.VMEM((TOKENS, x.shape[1]), BF16),
        pltpu.VMEM((HALO + 1, KV_HEADS, 2, TOKENS, HEAD_SIZE), BF16),
        pltpu.VMEM((TOKENS, KEYS), F32),
        pltpu.VMEM((TOKENS, features), BF16),
        pltpu.VMEM((2, 2 * NX * NY, RANK, PIECE), BF16),
        pltpu.VMEM((NZ, 2, COLS, PIECE), BF16),
        pltpu.VMEM((RANK, TOKENS), BF16),
        pltpu.VMEM((COLS, TOKENS), BF16),
        pltpu.VMEM((COLS, TOKENS), BF16),
        pltpu.VMEM((8, 2 * COLS), I32),
        pltpu.VMEM((NX * NY * RANK, 2 * COLS), BF16),
        pltpu.VMEM((NX * NY * RANK, 2 * COLS), BF16),
        pltpu.VMEM((8, COLS), I32),
        pltpu.VMEM((8, COLS), I32),
        pltpu.VMEM((PIECES, ring, COLS, PIECE), BF16),
        pltpu.VMEM((PIECES, ring, COLS, PIECE), BF16),
        pltpu.VMEM((PIECES, 2 * COLS, PIECE), BF16),
        pltpu.VMEM((by_y, NY - 1, NX * RANK, PIECE), BF16),
        pltpu.VMEM((by_y, NY - 1, NX * RANK, PIECE), BF16),
        pltpu.VMEM((by_x, NX - 1, NY * RANK, PIECE), BF16),
        pltpu.VMEM((by_x, NX - 1, NY * RANK, PIECE), BF16),
        pltpu.VMEM((by_y, NX - 1, RANK, PIECE), BF16),
        pltpu.VMEM((by_y, NX - 1, RANK, PIECE), BF16),
        pltpu.VMEM((by_x, NY - 1, RANK, PIECE), BF16),
        pltpu.VMEM((by_x, NY - 1, RANK, PIECE), BF16),
        pltpu.VMEM((by_y, NX * RANK, PIECE), F32),
        pltpu.VMEM((by_x, NY * RANK, PIECE), F32),
        dma((4 * KV_HEADS + 4,)),
        dma((2, KV_HEADS * HALO)),
        dma((2, 2 * NY)),
        dma((2, 2 * NX)),
        dma((2, 2)),
        dma((2, 2 * ring)),
        dma((2, PIECES, ring)),
        dma((2, PIECES)),
        dma((2, PIECES, ring)),
        dma((2, PIECES, ring)),
        dma((2, 1)),
    ]
    down, up = pl.pallas_call(
        kernel,
        out_shape=(
            jax.ShapeDtypeStruct((RANK, 2 * WIDTH), F32),
            jax.ShapeDtypeStruct((RANK, WIDTH), F32),
        ),
        in_specs=[hbm] * 7 + [smem] * 3,
        out_specs=(vmem, vmem),
        scratch_shapes=scratch,
        compiler_params=pltpu.CompilerParams(
            collective_id=0, has_side_effects=True, vmem_limit_bytes=60 * 1024 * 1024
        ),
    )(q, g, x, k, v, act.T, w, length, adapter, owner)
    return down.T[None], up[None]


def solution(mesh):
    return jax.shard_map(
        on_device,
        mesh=mesh,
        in_specs=(
            P(("seq", "head"), None),
            P(("seq", "head"), None),
            P(("seq", "head"), None),
            P(("seq", "head"), None),
            P(("seq", "head"), None),
            P(("seq", "head"), None),
            P("seq", None, "head"),
            P("seq", None),
            P("seq", None),
            P(),
        ),
        out_specs=(P("seq", "head", None), P("seq", None, "head")),
        check_vma=False,
    )
```

time: 138 us -> 117 us (0.85)
  the two profiles are of different devices: /device:TPU:64 before, /device:TPU:8 now
where the time goes in v2:
time: 117 us
  Pallas kernels  113 us (97%)
  local copies, waits for them, and re-layouts  2.85 us (2%)
    pallas_call x1, Pallas kernels, on_device(): pl.pallas_call(kernel, out_shape=(jax.ShapeDtypeStruct((RANK, 2 * WIDTH),...  113 us
    unnamed x2, local copies, waits for them, and re-layouts  2.85 us

profile of v2, /device:TPU:8, one launch (start us, length us, event | category | flops | bytes accessed | tf_op | source)
XLA Modules:
  0.0 116.9 jit_solution(4713306467090992605)
XLA Ops:
  0.6 113.4 %shard_map.113 = (f32[16,1024]{1,0:T(8,128)}, f32[16,512]{1,0:T(8,128)}) custom-call(bf16[128,4096]{1,0:T(8,128)(2,1)} %q_hbm.1, bf16[128,4096]{1,0:T(8,128)(2,1)} %g_hbm.1, bf16[128,8192]{1,0:T(8,128)(2,1)} %x_hbm.1, bf16[128,512]{1,0:T(8,128)(2,1)} %k_hbm.1, bf16[128,512]{1,0:T(8,128)(2,1)} %v_hbm.1, bf16[16,128]{1,0:T(8,128)(2,1)} %bitcast.7, ...), custom_call_target="tpu_custom_call" | custom-call | tf_op jit(solution)/shard_map/pallas_call | solution.py:538
  114.1 1.5 %copy.14 = f32[1,1024,16]{1,2,0:T(8,128)} copy(f32[1,1024,16]{1,2,0:T(8,128)} %bitcast.5) | data formatting | bytes 131072
  115.6 1.4 %copy.15 = f32[1,16,512]{2,1,0:T(8,128)} copy(f32[1,16,512]{2,1,0:T(8,128)} %bitcast.6) | data formatting | bytes 65536

commit v3 on v2

--- a/solution.py
+++ b/solution.py
@@ -24,8 +24,8 @@
 WIDTH = 512
 PIECE = 256
 PIECES = 6
-BEGIN = (-1, -1, 0, 0, 0, 0)
-Y_FIRST = (0, 2)
+BEGIN = (-1, -1, 0, 0, 1, 1)
+Y_FIRST = (0, 2, 4)
 ADAPTER_SCALE = 2.0
 SCORE_SCALE = 1.0 / HEAD_SIZE**0.5
 
@@ -210,6 +210,10 @@
         own_kv.append([load(src.at[:, lanes], kv.at[HALO, g, i]) for i, src in enumerate((k_hbm, v_hbm))])
     w_load = [load(w_hbm.at[0, :, pl.ds(h * PIECE, PIECE)], wall.at[h, places[h]]) for h in range(2)]
     act_load = load(act_hbm, act_v)
+    qg_load = []
+    for g in range(KV_HEADS):
+        lanes = pl.ds(g * GROUP * HEAD_SIZE, GROUP * HEAD_SIZE)
+        qg_load.append([load(src.at[:, lanes], dst.at[:, lanes]) for src, dst in ((q_hbm, qv), (g_hbm, gv))])
 
     sends = []
 
@@ -250,12 +254,8 @@
         [pass_w(0, places[0], wy_sem, d, at_y(d)) for d in range(1, NY)],
         [pass_w(1, places[1], wx_sem, d, at_x(d)) for d in range(1, NX)],
     ]
-    for g in range(KV_HEADS):
-        send_kv(g, 0)
-    qg_load = []
-    for g in range(KV_HEADS):
-        lanes = pl.ds(g * GROUP * HEAD_SIZE, GROUP * HEAD_SIZE)
-        qg_load.append([load(src.at[:, lanes], dst.at[:, lanes]) for src, dst in ((q_hbm, qv), (g_hbm, gv))])
+    send_kv(0, 0)
+    send_kv(1, 0)
 
     ends, total = [], 0
     for i in range(SEGMENTS):
@@ -335,22 +335,23 @@
         copy.wait_recv()
     row = pl.ds(mine + y * NX, NX)
     w_two = [None, [pass_w(1, row, wy_sem, NY + d, at_y(d)) for d in range(1, NY)]]
+    send_kv(0, 1)
+    send_kv(2, 0)
     for copy in w_one[0]:
         copy.wait_recv()
     row = pl.ds(mine + x * NY, NY)
     w_two[0] = [pass_w(0, row, wx_sem, NX + d, at_x(d)) for d in range(1, NX)]
-    for g in range(KV_HEADS):
-        send_kv(g, 1)
+    for g, d in ((1, 1), (3, 0), (0, 2), (2, 1), (1, 2)):
+        send_kv(g, d)
+    meta.wait_recv()
+    slots[:, COLS : 2 * COLS] = meta_r[...]
     w_core = []
     for h in range(2):
         for copy in w_two[h]:
             copy.wait_recv()
         w_core.append(pass_w(h, pl.ds(mine, NX * NY), wc_sem, h, partner))
-    for g in range(KV_HEADS):
-        send_kv(g, 2)
-    x_load = load(x_hbm, xv)
-    meta.wait_recv()
-    slots[:, COLS : 2 * COLS] = meta_r[...]
+    send_kv(3, 1)
+    send_kv(2, 2)
 
     wz_ways = ((1, 3, 0), (-1, 4, 3))
     wz_copies = {}
@@ -366,12 +367,16 @@
                         wz.at[at, h], wz.at[at, h], wz_sem, h * (NZ - 1) + base + step, at_z(sign)
                     )
 
+    attend(0)
+    send_kv(3, 2)
     every = lax.broadcasted_iota(I32, (COLS, 2 * NX * NY * RANK), 1)
     for h in range(2):
         w_core[h].wait_recv()
         pick = jnp.where(every == col_rows[h], 1.0, 0.0).astype(BF16)
         wz[z, h] = nn(pick, wall[h].reshape(2 * NX * NY * RANK, PIECE)).astype(BF16)
         pass_on(h, 0)
+    x_load = load(x_hbm, xv)
+
     def fill(i, carry):
         row = i * (NX * RANK) + lax.broadcasted_iota(I32, (NX * RANK, 2 * COLS), 0)
         low = core * RANK + lax.rem(row, RANK)
@@ -383,11 +388,10 @@
         return carry
 
     lax.fori_loop(0, NY, fill, 0)
-    for g in range(KV_HEADS):
+    for g in range(1, KV_HEADS):
         attend(g)
-        if g < 3:
-            for h in range(2):
-                pass_on(h, g + 1)
+        for h in range(2):
+            pass_on(h, g)
 
     def zcols(ref, c, i, width):
         return ref[:, pl.ds(pl.multiple_of(c * width + i * PIECE, PIECE), PIECE)]
@@ -433,7 +437,7 @@
         else:
             held.append(tx.at[at])
             f_sums.append(
-                RingSum(NX, x, at_x, functools.partial(x_chunk, p), *refs(p, at, fxs, fxr, f_sem), 1 + p % 2)
+                DirectSum(NX, x, at_x, functools.partial(x_chunk, p), *refs(p, at, fxs, fxr, f_sem))
             )
             s_sums.append(
                 DirectSum(NY, y, at_y, functools.partial(rows_of, tx.at[at]), *refs(p, at, sys_, syr, s_sem))
@@ -456,13 +460,13 @@
         ref[:, at * PIECE : (at + 1) * PIECE] = s_sums[p].final() * ADAPTER_SCALE
 
     def rank_all():
-        for h in range(2):
-            pass_on(h, 4)
         rank = jnp.zeros((COLS, TOKENS), F32)
-        for c in range(NZ):
+        for d in (0, -1, 1, -2, 2, -3, 3, 4):
+            c = lax.rem(z + d + NZ, NZ)
             for h in range(2):
-                at = c * WIDTH + h * PIECE
-                rank = rank + nt(wz[c, h], dq[:, at : at + PIECE])
+                if d == 4:
+                    pass_on(h, 4)
+                rank = rank + nt(wz[c, h], zcols(dq, c, h, WIDTH))
         rank_cols[...] = jnp.where(mask, rank, 0.0).astype(BF16)
         x_load.wait()
 
@@ -470,10 +474,12 @@
     for p, begin in enumerate(BEGIN):
         steps = [functools.partial(z_sums[p].stage, i) for i in range(4)]
         steps += [functools.partial(to_partner, p), functools.partial(first_hop, p)]
-        if p not in Y_FIRST:
-            steps.append(functools.partial(f_sums[p].stage, 1))
         steps += [functools.partial(turn, p), functools.partial(write, p)]
-        plan += [(begin + i, 0 if i < 5 else 1, p, step) for i, step in enumerate(steps)]
+        late = (1, 2, 2) if begin == 0 else (1, 1, 1)
+        when = [(begin + i, (0.5 if begin < 0 else 0, 0 if begin >= 0 else 0.5, 0 if begin >= 0 else 0.5, 0 if begin >= 0 else 0.5, 2, *late)[i]) for i in range(8)]
+        if begin < 0:
+            when[6:] = [(6, 3), (8, 0)]
+        plan += [(*at, p, step) for at, step in zip(when, steps)]
     plan.append((0, -1, 0, rank_all))
     for _, _, _, step in sorted(plan, key=lambda entry: entry[:3]):
         step()

time: 117 us -> 110 us (0.940)
  the two profiles are of different devices: /device:TPU:8 before, /device:TPU:4 now
where the time goes in v3:
time: 110 us
  Pallas kernels  107 us (97%)
  local copies, waits for them, and re-layouts  2.85 us (3%)
    pallas_call x1, Pallas kernels, on_device(): pl.pallas_call(kernel, out_shape=(jax.ShapeDtypeStruct((RANK, 2 * WIDTH),...  107 us
    unnamed x2, local copies, waits for them, and re-layouts  2.85 us

profile of v3, /device:TPU:4, one launch (start us, length us, event | category | flops | bytes accessed | tf_op | source)
XLA Modules:
  0.0 110.1 jit_solution(9296253170414066298)
XLA Ops:
  0.6 106.6 %shard_map.113 = (f32[16,1024]{1,0:T(8,128)}, f32[16,512]{1,0:T(8,128)}) custom-call(bf16[128,4096]{1,0:T(8,128)(2,1)} %q_hbm.1, bf16[128,4096]{1,0:T(8,128)(2,1)} %g_hbm.1, bf16[128,8192]{1,0:T(8,128)(2,1)} %x_hbm.1, bf16[128,512]{1,0:T(8,128)(2,1)} %k_hbm.1, bf16[128,512]{1,0:T(8,128)(2,1)} %v_hbm.1, bf16[16,128]{1,0:T(8,128)(2,1)} %bitcast.7, ...), custom_call_target="tpu_custom_call" | custom-call | tf_op jit(solution)/shard_map/pallas_call | solution.py:544
  107.3 1.5 %copy.14 = f32[1,1024,16]{1,2,0:T(8,128)} copy(f32[1,1024,16]{1,2,0:T(8,128)} %bitcast.5) | data formatting | bytes 131072
  108.7 1.4 %copy.15 = f32[1,16,512]{2,1,0:T(8,128)} copy(f32[1,16,512]{2,1,0:T(8,128)} %bitcast.6) | data formatting | bytes 65536

commit v4 on v3

--- a/solution.py
+++ b/solution.py
@@ -16,6 +16,7 @@
 GROUP = 8
 RANK = 16
 PAIR = 2
+FAR = 2
 SEGMENTS = 8
 COLS = SEGMENTS * RANK
 TOKENS = 128
@@ -24,7 +25,7 @@
 WIDTH = 512
 PIECE = 256
 PIECES = 6
-BEGIN = (-1, -1, 0, 0, 1, 1)
+BEGIN = (-2, -2, 0, 0, 1, 1)
 Y_FIRST = (0, 2, 4)
 ADAPTER_SCALE = 2.0
 SCORE_SCALE = 1.0 / HEAD_SIZE**0.5
@@ -188,7 +189,8 @@
 
     barrier = pltpu.get_barrier_semaphore()
     others = (
-        [at_z(1), at_z(-1), partner]
+        [at_z(d) for d in (1, -1, 2, -2)]
+        + [partner]
         + [at_y(d) for d in range(1, NY)]
         + [at_x(d) for d in range(1, NX)]
     )
@@ -353,19 +355,22 @@
     send_kv(3, 1)
     send_kv(2, 2)
 
-    wz_ways = ((1, 3, 0), (-1, 4, 3))
     wz_copies = {}
 
-    def pass_on(h, step):
-        for sign, hops, base in wz_ways:
-            if step <= hops:
-                if step > 0:
-                    wz_copies[h, base + step - 1].wait_recv()
-                if step < hops:
-                    at = lax.rem(z - sign * step + NZ, NZ)
-                    wz_copies[h, base + step] = remote(
-                        wz.at[at, h], wz.at[at, h], wz_sem, h * (NZ - 1) + base + step, at_z(sign)
-                    )
+    def pass_wz(h, at, origin, to):
+        rows = lax.rem(z + origin + NZ, NZ)
+        wz_copies[h, at] = remote(wz.at[rows, h], wz.at[rows, h], wz_sem, h * (NZ - 1) + at, at_z(to))
+
+    def spread_near(h):
+        for at, to in enumerate((2, -2, 1, -1)):
+            pass_wz(h, at, 0, to)
+
+    def spread_far(h):
+        for at in range(2):
+            wz_copies[h, at].wait_recv()
+        pass_wz(h, 4, -2, 1)
+        pass_wz(h, 5, 2, -1)
+        pass_wz(h, 6, 4 * h - 2, 2 - 4 * h)
 
     attend(0)
     send_kv(3, 2)
@@ -374,7 +379,7 @@
         w_core[h].wait_recv()
         pick = jnp.where(every == col_rows[h], 1.0, 0.0).astype(BF16)
         wz[z, h] = nn(pick, wall[h].reshape(2 * NX * NY * RANK, PIECE)).astype(BF16)
-        pass_on(h, 0)
+        spread_near(h)
     x_load = load(x_hbm, xv)
 
     def fill(i, carry):
@@ -390,8 +395,9 @@
     lax.fori_loop(0, NY, fill, 0)
     for g in range(1, KV_HEADS):
         attend(g)
-        for h in range(2):
-            pass_on(h, g)
+        if g == FAR:
+            for h in range(2):
+                spread_far(h)
 
     def zcols(ref, c, i, width):
         return ref[:, pl.ds(pl.multiple_of(c * width + i * PIECE, PIECE), PIECE)]
@@ -461,11 +467,11 @@
 
     def rank_all():
         rank = jnp.zeros((COLS, TOKENS), F32)
-        for d in (0, -1, 1, -2, 2, -3, 3, 4):
+        for d, at in ((0, None), (-2, None), (2, None), (-1, 2), (1, 3), (-3, 4), (3, 5), (4, 6)):
             c = lax.rem(z + d + NZ, NZ)
             for h in range(2):
-                if d == 4:
-                    pass_on(h, 4)
+                if at is not None:
+                    wz_copies[h, at].wait_recv()
                 rank = rank + nt(wz[c, h], zcols(dq, c, h, WIDTH))
         rank_cols[...] = jnp.where(mask, rank, 0.0).astype(BF16)
         x_load.wait()

time: 110 us -> 110 us (level)
  the two profiles are of different devices: /device:TPU:4 before, /device:TPU:1 now
where the time goes in v4:
time: 110 us; the launch traced here: 109 us
  Pallas kernels  106 us (96%)
  local copies, waits for them, and re-layouts  2.85 us (3%)
    pallas_call x1, Pallas kernels, on_device(): pl.pallas_call(kernel, out_shape=(jax.ShapeDtypeStruct((RANK, 2 * WIDTH),...  106 us
    unnamed x2, local copies, waits for them, and re-layouts  2.85 us

profile of v4, /device:TPU:1, one launch (start us, length us, event | category | flops | bytes accessed | tf_op | source)
XLA Modules:
  0.0 109.4 jit_solution(13663549555528295135)
XLA Ops:
  0.6 105.9 %shard_map.113 = (f32[16,1024]{1,0:T(8,128)}, f32[16,512]{1,0:T(8,128)}) custom-call(bf16[128,4096]{1,0:T(8,128)(2,1)} %q_hbm.1, bf16[128,4096]{1,0:T(8,128)(2,1)} %g_hbm.1, bf16[128,8192]{1,0:T(8,128)(2,1)} %x_hbm.1, bf16[128,512]{1,0:T(8,128)(2,1)} %k_hbm.1, bf16[128,512]{1,0:T(8,128)(2,1)} %v_hbm.1, bf16[16,128]{1,0:T(8,128)(2,1)} %bitcast.7, ...), custom_call_target="tpu_custom_call" | custom-call | tf_op jit(solution)/shard_map/pallas_call | solution.py:550
  106.6 1.5 %copy.14 = f32[1,1024,16]{1,2,0:T(8,128)} copy(f32[1,1024,16]{1,2,0:T(8,128)} %bitcast.5) | data formatting | bytes 131072
  108.0 1.4 %copy.15 = f32[1,16,512]{2,1,0:T(8,128)} copy(f32[1,16,512]{2,1,0:T(8,128)} %bitcast.6) | data formatting | bytes 65536
